TPU v7x, 256 devices: a whole 4x4x8 slice. The times are simulated.
256 devices in a mesh: ctx: 64 (over y, z, x_lo), head: 4 (over x_hi, core).
Axes of the slice: x: 4 (x_hi: 2, x_lo: 2; x = x_hi * 2 + x_lo), y: 4, z: 8, core: 2. Of those that a mesh axis runs over, the one named last changes fastest.
Arguments:
- queries: bfloat16 [16384, 1024], P(('ctx', 'head')), may hold values from -7 to 7
- key_vecs: bfloat16 [16384, 128], P(('ctx', 'head')), may hold values from -7 to 7
- value_vecs: bfloat16 [16384, 128], P(('ctx', 'head')), may hold values from -6 to 6
- out_grad: bfloat16 [16384, 1024], P(('ctx', 'head')), may hold values from -192 to 192
Outputs:
- query_grad: bfloat16 [16384, 1024], P(('ctx', 'head'))
- key_grad: bfloat16 [16384, 128], P(('ctx', 'head'))
- value_grad: bfloat16 [16384, 128], P(('ctx', 'head'))
All inputs are finite; a program needn't handle non-finite values.
Results may differ from a plain program's by a relative error of at most 0.035.
Values may be sent and summed in bfloat16 or wider, within the bound.
A program may use at most 128 MiB of HBM per device.

v0:
```python
import jax
import jax.numpy as jnp
from jax import lax
from jax.sharding import PartitionSpec as P


def row_block(total_rows):
    block_rows = min(total_rows, 2048)
    while total_rows % block_rows != 0:
        block_rows = block_rows - 1
    return block_rows


def over_blocks(kernel, running, arrays):
    total_rows = arrays[0].shape[0]
    block_rows = row_block(total_rows)
    blocks = total_rows // block_rows
    stacked = tuple((member.reshape((blocks, block_rows) + member.shape[1:]) for member in arrays))
    running, results = lax.scan(kernel, running, stacked)
    if results is not None:
        results = results.reshape((total_rows,) + results.shape[2:])
    return (running, results)


def forward_kernel(queries_loc, scaling):

    def kernel(running, arrays):
        key_part, value_part = arrays
        maxima, totals, weighted = running
        scores = (
            jnp.einsum("qhd,kd->hqk", queries_loc, key_part, preferred_element_type=jnp.float32)
            * scaling
        )
        newmax = jnp.maximum(maxima, jnp.max(scores, axis=2))
        weights = jnp.exp(scores - newmax[:, :, None])
        factor = jnp.exp(maxima - newmax)
        totals = totals * factor + jnp.sum(weights, axis=2)
        weighted = weighted * factor[:, :, None] + jnp.einsum(
            "hqk,kd->hqd",
            weights.astype(jnp.bfloat16),
            value_part,
            preferred_element_type=jnp.float32,
        )
        return ((newmax, totals, weighted), None)

    return kernel


def backward_kernel(queries_loc, grads_loc, log_totals, row_dots, scaling):

    def kernel(running, arrays):
        key_part, value_part = arrays
        scores = (
            jnp.einsum("qhd,kd->hqk", queries_loc, key_part, preferred_element_type=jnp.float32)
            * scaling
        )
        chances = jnp.exp(scores - log_totals[:, :, None])
        prob_grad = jnp.einsum(
            "qhd,kd->hqk", grads_loc, value_part, preferred_element_type=jnp.float32
        )
        score_grad = (chances * (prob_grad - row_dots[:, :, None])).astype(jnp.bfloat16)
        running = running + jnp.einsum(
            "hqk,kd->qhd", score_grad, key_part, preferred_element_type=jnp.float32
        )
        key_term = jnp.einsum(
            "hqk,qhd->kd", score_grad, queries_loc, preferred_element_type=jnp.float32
        )
        value_term = jnp.einsum(
            "hqk,qhd->kd",
            chances.astype(jnp.bfloat16),
            grads_loc,
            preferred_element_type=jnp.float32,
        )
        return (running, jnp.concatenate([key_term, value_term], axis=1))

    return kernel


def body(queries, key_vecs, value_vecs, out_grad):
    head_size = key_vecs.shape[1]
    scaling = head_size ** (-0.5)
    moved_queries, moved_grads = (
        lax.all_to_all(queries, "head", split_axis=1, concat_axis=0, tiled=True),
        lax.all_to_all(out_grad, "head", split_axis=1, concat_axis=0, tiled=True),
    )
    block_len = moved_queries.shape[0]
    local_heads = moved_queries.shape[1] // head_size
    queries_loc = moved_queries.reshape(block_len, local_heads, head_size)
    grads_loc = moved_grads.reshape(block_len, local_heads, head_size)
    start_state = (
        jnp.full((local_heads, block_len), -1e30, jnp.float32),
        jnp.zeros((local_heads, block_len), jnp.float32),
        jnp.zeros((local_heads, block_len, head_size), jnp.float32),
    )
    forward = forward_kernel(queries_loc, scaling)
    keys_all, values_all = (
        lax.all_gather(key_vecs, ("ctx", "head"), axis=0, tiled=True),
        lax.all_gather(value_vecs, ("ctx", "head"), axis=0, tiled=True),
    )
    maxima, totals, weighted = over_blocks(forward, start_state, (keys_all, values_all))[0]
    log_totals = maxima + jnp.log(totals)
    attended = (weighted / totals[:, :, None]).astype(jnp.bfloat16)
    row_dots = jnp.einsum("qhd,hqd->hq", grads_loc, attended, preferred_element_type=jnp.float32)
    query_zero = jnp.zeros((block_len, local_heads, head_size), jnp.float32)
    both_kernel = backward_kernel(queries_loc, grads_loc, log_totals, row_dots, scaling)
    query_acc, key_sums = over_blocks(both_kernel, query_zero, (keys_all, values_all))
    summed = lax.psum_scatter(key_sums, ("ctx", "head"), scatter_dimension=0, tiled=True)
    query_low = (
        (query_acc * scaling).astype(jnp.bfloat16).reshape(block_len, local_heads * head_size)
    )
    query_grad = lax.all_to_all(query_low, "head", split_axis=0, concat_axis=1, tiled=True)
    key_grad = (summed[:, :head_size] * scaling).astype(jnp.bfloat16)
    value_grad = summed[:, head_size:].astype(jnp.bfloat16)
    return (query_grad, key_grad, value_grad)


def solution(mesh):
    return jax.shard_map(
        body,
        mesh=mesh,
        in_specs=(
            P(("ctx", "head"), None),
            P(("ctx", "head"), None),
            P(("ctx", "head"), None),
            P(("ctx", "head"), None),
        ),
        out_specs=(P(("ctx", "head"), None), P(("ctx", "head"), None), P(("ctx", "head"), None)),
        check_vma=False,
    )
```

profile of v0, /device:TPU:1, one launch (start us, length us, event | category | flops | bytes accessed | tf_op | source)
XLA Modules:
  0.0 2271.7 jit_solution(18069915502302481624)
XLA Ops:
  10.2 6.5 all-to-all-start
  18.3 3.6 all-to-all-done
  21.9 4.3 all-to-all-start.1
  26.4 5.0 all-to-all-done.1
  31.5 395.3 %all-gather.3.cloned.1.call-done = bf16[16384,128]{1,0:T(8,128)(2,1)} async-done(((bf16[64,128]{1,0:T(8,128)(2,1)}), bf16[16384,128]{1,0:T(8,128)(2,1)}) %all-gather.3.cloned.1.call-update) | async-done | bytes 4194320 | tf_op jit(solution)/shard_map/all_gather | solution.py:97
  426.8 413.4 %all-gather.5.cloned.1.call-done = bf16[16384,128]{1,0:T(8,128)(2,1)} async-done(((bf16[64,128]{1,0:T(8,128)(2,1)}), bf16[16384,128]{1,0:T(8,128)(2,1)}) %all-gather.5.cloned.1.call-update) | async-done | bytes 4194320 | tf_op jit(solution)/shard_map/all_gather | solution.py:98
  840.2 35.9 %while.28 = (s32[]{:T(128)}, f32[2,256]{1,0:T(2,128)S(1)}, f32[2,256]{1,0:T(2,128)S(1)}, f32[2,256,128]{2,1,0:T(8,128)S(1)}, bf16[8,2048,128]{2,1,0:T(8,128)(2,1...) while((s32[]{:T(128)}, f32[2,256]{1,0:T(2,128)S(1)}, ...), condition=%wide.region_3.4_spmd.clone, body=%wide.region_0.3_spmd.clone.sunk | while | flops 545458688 | bytes 14319737 | solution.py:19
  840.2 1.8 bitcast_reduce_fusion.2
  842.7 2.0 fusion.74
  844.7 1.8 bitcast_reduce_fusion.2
  847.2 2.0 fusion.74
  849.2 1.8 bitcast_reduce_fusion.2
  851.7 2.0 fusion.74
  853.7 1.8 bitcast_reduce_fusion.2
  856.2 2.0 fusion.74
  858.2 1.8 bitcast_reduce_fusion.2
  860.7 2.0 fusion.74
  862.7 1.8 bitcast_reduce_fusion.2
  865.2 2.0 fusion.74
  867.2 1.8 bitcast_reduce_fusion.2
  869.7 2.0 fusion.74
  871.7 1.8 bitcast_reduce_fusion.2
  874.2 2.0 fusion.74
  876.8 96.6 %while.29 = (s32[]{:T(128)}, f32[256,2,128]{0,2,1:T(8,128)S(1)}, f32[8,2048,256]{2,1,0:T(8,128)}, bf16[8,2048,128]{2,1,0:T(8,128)(2,1)}, bf16[256,2,128]{0,2,1:T...) while((s32[]{:T(128)}, f32[256,2,128]{0,2,1:T(8,128)S(1)}, ...), condition=%wide.region_5.6_spmd.clone, body=%wide.region_4.5_spmd.clone.sunk | while | flops 1351221248 | bytes 36182160 | solution.py:19
  876.8 1.7 fusion.85
  879.4 2.1 fusion.86
  885.4 1.9 copy.73
  888.8 1.7 fusion.85
  891.5 2.1 fusion.86
  897.5 1.9 copy.73
  900.9 1.7 fusion.85
  903.6 2.1 fusion.86
  909.6 1.9 copy.73
  912.9 1.7 fusion.85
  915.6 2.1 fusion.86
  921.6 1.9 copy.73
  925.0 1.7 fusion.85
  927.7 2.1 fusion.86
  933.7 1.9 copy.73
  937.1 1.7 fusion.85
  939.8 2.1 fusion.86
  945.8 1.9 copy.73
  951.9 2.1 fusion.86
  957.9 1.9 copy.73
  963.9 2.1 fusion.86
  969.9 1.9 copy.73
  973.6 10.6 all_to_all.51
  984.8 1277.6 %reduce-scatter.2.cloned.1.call-done = f32[64,256]{1,0:T(8,128)} async-done(((f32[16384,256]{1,0:T(8,128)}), f32[64,256]{1,0:T(8,128)}) %reduce-scatter.2.cloned.1.call-update) | async-done | bytes 65552 | tf_op jit(solution)/shard_map/reduce_scatter | solution.py:107
  (102 shorter events, 68.7 us)
Async XLA Ops:
  7.2 419.7 %all-gather.3.cloned.1.call-start = ((), (), s32[]{:S(2)}) async-start(), calls=%async_computation.4 | async-start | bytes 4210688 | tf_op jit(solution)/shard_map/all_gather | solution.py:97
  7.9 832.3 %all-gather.5.cloned.1.call-start = ((), (), s32[]{:S(2)}) async-start(), calls=%async_computation.5 | async-start | bytes 4210688 | tf_op jit(solution)/shard_map/all_gather | solution.py:98
  10.2 11.6 all-to-all-start
  21.9 9.5 all-to-all-start.1
  26.2 2236.2 %reduce-scatter.2.cloned.1.call-start = ((), (), s32[]{:S(2)}) async-start(), calls=%async_computation.6 | async-start | bytes 16842752 | tf_op jit(solution)/shard_map/reduce_scatter | solution.py:107
Sparse Core Ops, SparseCore 0:
  9.9 416.8 all-gather.2
  428.7 411.4 all-gather.4
  973.5 1288.9 reduce-scatter.1
where the time goes:
time: 2280 us; the launch traced here: 2270 us
  waiting for transfers between devices  2100 us (92%)
  matrix products  86.7 us (4%)
  local copies, waits for them, and re-layouts  32.9 us (1%)
    reduce_scatter x1, waiting for transfers between devices, body(): lax.psum_scatter(key_sums, ('ctx', 'head'), scatter_dimension=0, tiled=True)  1280 us
    all_gather x1, waiting for transfers between devices, body(): lax.all_gather(value_vecs, ('ctx', 'head'), axis=0, tiled=True)  413 us
    all_gather x1, waiting for transfers between devices, body(): lax.all_gather(key_vecs, ('ctx', 'head'), axis=0, tiled=True)  395 us
  transfers between devices with their start and end apart: 5, of which 5 were waited for; matrix products, arithmetic and copies ran while one was open for 0% of the time, Pallas kernels for 0%

commit v1 on v0

v1 whole, which is shorter than its diff:
```python
import math

import jax
import jax.numpy as jnp
from jax import lax
from jax.experimental import pallas as pl
from jax.experimental.pallas import tpu as pltpu
from jax.sharding import PartitionSpec as P

F32, BF16 = jnp.float32, jnp.bfloat16
MESH = pl.DeviceIdType.MESH
NX, NY, NZ = 4, 4, 8
TOK = 64
DIM = 128
HALF = 512
RB = 512
KT = 1024
ROWS, KEYS = NX * RB, NY * KT
OFF = (0, 1, 3, 2)
SLOT = (0, 1, 3, 2)
SCALE = DIM**-0.5
LOG2_SCALE = SCALE * math.log2(math.e)
Z_ORDER = (1, 7, 2, 6, 3, 5, 4)


def nt(a, b):
    return lax.dot_general(a, b, (((1,), (1,)), ((), ())), preferred_element_type=F32)


def nn(a, b):
    return jnp.dot(a, b, preferred_element_type=F32)


def kernel(
    q_in, do_in, k_in, v_in, dq_out, dk_out, dv_out,
    qb, dob, kvb, kt, vt, w, mt, acc, st, sr, lse, rdn, fcol, dqt, dkv,
    sib_src, sib, r2_src, r2, y_src, yr, z_src, zr, dq_src, dqr,
    loc_sem, q_ss, q_rs, z_ss, z_rs, sb_ss, sb_rs, yk_ss, yk_rs, y2_ss, y2_rs,
    st_ss, st_rs, sib_ss, sib_rs, r2_ss, r2_rs, yr_ss, yr_rs, zr_ss, zr_rs, dq_ss, dq_rs,
):
    ctx, hd = lax.axis_index("ctx"), lax.axis_index("head")
    y, z = ctx // (2 * NZ), lax.rem(ctx // 2, NZ)
    x, c = (hd // 2) * 2 + lax.rem(ctx, 2), lax.rem(hd, 2)

    def dev(dx=0, dy=0, dz=0, dc=0):
        xx, yy = lax.rem(x + dx, NX), lax.rem(y + dy, NY)
        zz, cc = lax.rem(z + dz, NZ), lax.rem(c + dc, 2)
        return ((yy * NZ + zz) * 2 + lax.rem(xx, 2), (xx // 2) * 2 + cc)

    pending = []

    def send(src, dst, ss, rs, to):
        copy = pltpu.make_async_remote_copy(
            src_ref=src, dst_ref=dst, send_sem=ss, recv_sem=rs,
            device_id=to, device_id_type=MESH,
        )
        copy.start()
        pending.append(copy)

    def arrive(ref, rs):
        pltpu.make_async_remote_copy(
            src_ref=ref, dst_ref=ref, send_sem=rs, recv_sem=rs,
            device_id=dev(dc=1), device_id_type=MESH,
        ).wait_recv()

    def zrow(dz, core=0):
        zz = lax.rem(z + (NZ - dz), NZ)
        return pl.ds(pl.multiple_of(core * (NZ * TOK) + zz * TOK, TOK), TOK)

    def half(dc):
        return pl.ds(pl.multiple_of(lax.rem(c + dc, 2) * HALF, HALF), HALF)

    own = [
        pltpu.make_async_copy(k_in, kvb.at[0, zrow(0), 0:DIM], loc_sem.at[0]),
        pltpu.make_async_copy(v_in, kvb.at[0, zrow(0), DIM : 2 * DIM], loc_sem.at[1]),
        pltpu.make_async_copy(q_in.at[:, half(0)], qb.at[0, 0], loc_sem.at[2]),
        pltpu.make_async_copy(do_in.at[:, half(0)], dob.at[0, 0], loc_sem.at[3]),
    ]
    for copy in own:
        copy.start()
    xc = [(dx, dc) for dx in range(NX) for dc in range(2) if (dx, dc) != (0, 0)]
    partners = [dev(dx=dx, dc=dc) for dx, dc in xc]
    partners += [dev(dz=dz) for dz in range(1, NZ)] + [dev(dy=1), dev(dy=3)]
    barrier = pltpu.get_barrier_semaphore()
    for to in partners:
        pl.semaphore_signal(barrier, inc=1, device_id=to, device_id_type=MESH)
    pl.semaphore_wait(barrier, len(partners))
    for copy in own:
        copy.wait()

    mine = kvb.at[0, zrow(0)]
    for dz in Z_ORDER:
        send(mine, mine, z_ss.at[dz], z_rs.at[dz], dev(dz=dz))
    for dx, dc in sorted(xc, key=lambda m: (m[0] != 0, m[0] == 2)):
        slot = SLOT[(NX - dx) % NX]
        for i, (src, dst) in enumerate(((q_in, qb), (do_in, dob))):
            send(src.at[:, half(dc)], dst.at[slot, dc], q_ss.at[dx, dc, i], q_rs.at[slot, dc, i], dev(dx=dx, dc=dc))

    def spread(dz):
        block = kvb.at[0, zrow(dz)]
        send(block, kvb.at[0, zrow(dz, 1)], sb_ss.at[0, dz], sb_rs.at[0, dz], dev(dc=1))
        send(block, kvb.at[2, zrow(dz)], yk_ss.at[0, dz], yk_rs.at[0, dz], dev(dy=1))
        send(block, kvb.at[1, zrow(dz)], yk_ss.at[1, dz], yk_rs.at[1, dz], dev(dy=3))

    spread(0)
    for dz in Z_ORDER:
        arrive(kvb.at[0, zrow(dz)], z_rs.at[dz])
        spread(dz)

    def transposed(t):
        for i in range(2):
            rows, cols = pl.ds(i * 512, 512), pl.ds(t * KT + i * 512, 512)
            kt[:, cols] = kvb[t, rows, 0:DIM].T
            vt[0:DIM, cols] = kvb[t, rows, DIM : 2 * DIM].T

    def rows_of(ref, xo):
        return jnp.concatenate(
            [ref[xo, a, :, h * DIM : (h + 1) * DIM] for a in range(2) for h in range(4)], axis=0
        )

    def lanes(xo):
        return pl.ds(pl.multiple_of(xo * RB, RB), RB)

    def forward(xo, tiles, first=False):
        rows = lanes(xo)
        qs = rows_of(qb, xo)
        if not first:
            top, total = st[xo, 0:1, :], acc[:, rows]
        for t in tiles:
            s = nt(kvb[t, :, 0:DIM], qs)
            m = jnp.max(s, axis=0, keepdims=True) * LOG2_SCALE
            p = jnp.exp2(s * LOG2_SCALE - m).astype(BF16)
            w[pl.ds(t * KT, KT), rows] = p
            mt[t : t + 1, rows] = m
            a = nn(vt[:, t * KT : (t + 1) * KT], p)
            if first:
                top, total, first = m, a, False
            else:
                new = jnp.maximum(top, m)
                total = total * jnp.exp2(top - new) + a * jnp.exp2(m - new)
                top = new
        st[xo, 0:1, :] = top
        acc[:, rows] = total

    vt[DIM : DIM + 16, :] = jnp.ones((16, KEYS), BF16)
    mt[...] = jnp.zeros_like(mt)
    st[...] = jnp.zeros_like(st)
    for dz in (0,) + Z_ORDER:
        arrive(kvb.at[0, zrow(dz, 1)], sb_rs.at[0, dz])
    transposed(0)

    def arrive_rows(slot):
        for dc in range(2):
            if (slot, dc) != (0, 0):
                arrive(qb.at[slot, dc], q_rs.at[slot, dc, 0])
                arrive(dob.at[slot, dc], q_rs.at[slot, dc, 1])

    for slot in range(NX):
        arrive_rows(slot)

    def first_tile(xo, carry):
        forward(xo, (0,), True)
        return carry

    lax.fori_loop(0, 2, first_tile, 0)

    for n, dz in enumerate((0,) + Z_ORDER):
        for i, t in ((0, 2), (1, 1)):
            block = kvb.at[t, zrow(dz)]
            arrive(block, yk_rs.at[i, dz])
            send(block, kvb.at[t, zrow(dz, 1)], sb_ss.at[t, dz], sb_rs.at[t, dz], dev(dc=1))
            if n % 2 == i:
                send(block, kvb.at[3, zrow(dz)], y2_ss.at[dz], y2_rs.at[dz], dev(dy=1 if i == 0 else 3))

    lax.fori_loop(2, 4, first_tile, 0)

    for dz in (0,) + Z_ORDER:
        block = kvb.at[3, zrow(dz)]
        arrive(block, y2_rs.at[dz])
        send(block, kvb.at[3, zrow(dz, 1)], sb_ss.at[3, dz], sb_rs.at[3, dz], dev(dc=1))
    for t in (1, 2):
        for dz in (0,) + Z_ORDER:
            arrive(kvb.at[t, zrow(dz, 1)], sb_rs.at[t, dz])
        transposed(t)

    def middle_tiles(xo, carry):
        forward(xo, (1, 2))
        return carry

    lax.fori_loop(0, NX, middle_tiles, 0)
    for dz in (0,) + Z_ORDER:
        arrive(kvb.at[3, zrow(dz, 1)], sb_rs.at[3, dz])
    transposed(3)
    for xo in range(NX):
        forward(xo, (3,))
        rows = lanes(xo)
        st[xo, 1:2, :] = acc[DIM : DIM + 1, rows]
        grads = rows_of(dob, xo).astype(F32).T
        st[xo, 2:3, :] = jnp.sum(grads * acc[0:DIM, rows], axis=0, keepdims=True)
        for dx in (1, 3, 2):
            seen = SLOT[(NX - dx) % NX] - 1
            send(st.at[xo], sr.at[seen, xo], st_ss.at[dx - 1, xo], st_rs.at[seen, xo], dev(dx=dx))

    def totals(xo):
        rows = lanes(xo)
        parts = [st[xo]]
        for p in range(3):
            theirs = SLOT[(OFF[xo] - OFF[p + 1]) % NX]
            arrive(sr.at[p, theirs], st_rs.at[p, theirs])
            parts.append(sr[p, theirs])
        top = parts[0][0:1]
        for part in parts[1:]:
            top = jnp.maximum(top, part[0:1])
        total, dot = 0.0, 0.0
        for part in parts:
            factor = jnp.exp2(part[0:1] - top)
            total += part[1:2] * factor
            dot += part[2:3] * factor
        log_total = top + jnp.log2(total)
        lse[0:1, rows] = log_total
        rdn[0:1, rows] = dot / total
        f = jnp.exp2(mt[:, rows] - log_total)
        for i in range(RB // 128):
            part = jnp.concatenate([f[:, i * 128 : (i + 1) * 128], jnp.zeros((120, 128), F32)], axis=0)
            fcol[xo, i * 128 : (i + 1) * 128, :] = part.T

    def backward(xo, t, start):
        rows = lanes(xo)
        f = jnp.exp2(mt[t : t + 1, rows] - lse[0:1, rows])
        grads = (rows_of(dob, xo).astype(F32) * fcol[xo, :, t : t + 1]).astype(BF16)
        p = w[pl.ds(t * KT, KT), rows]
        pg = nt(kvb[t, :, DIM : 2 * DIM], grads) - f * rdn[0:1, rows]
        ds = p * pg.astype(BF16)
        dkv[t, :, DIM : 2 * DIM] += nn(p, grads)
        dkv[t, :, 0:DIM] += nn(ds, rows_of(qb, xo))
        d = nn(kt[:, t * KT : (t + 1) * KT], ds)
        if start:
            dqt[:, rows] = d
        else:
            dqt[:, rows] += d

    def loop(t, lo, hi):
        def step(xo, carry):
            backward(xo, t, False)
            return carry

        lax.fori_loop(lo, hi, step, 0, unroll=True)

    OWN = NZ * TOK
    factor = jnp.where(lax.broadcasted_iota(jnp.int32, (1, 2 * DIM), 1) < DIM, SCALE, 1.0)

    def to_sibling(t):
        sib_src[t] = (dkv[t, OWN:, :] * factor).astype(BF16)
        send(sib_src.at[t], sib.at[t], sib_ss.at[t], sib_rs.at[t], dev(dc=1))

    def chip_sum(t):
        arrive(sib.at[t], sib_rs.at[t])
        return dkv[t, 0:OWN, :] * factor + sib[t].astype(F32)

    H = OWN // 2
    for t in range(NY):
        dkv[t] = jnp.zeros((KT, 2 * DIM), F32)
    for xo in range(NX):
        totals(xo)
        backward(xo, 3, True)
    to_sibling(3)
    loop(1, 0, 2)
    r2_src[...] = chip_sum(3).astype(BF16)
    send(r2_src.at[0:H], r2.at[0], r2_ss.at[0], r2_rs.at[0], dev(dy=1))
    send(r2_src.at[H:], r2.at[1], r2_ss.at[1], r2_rs.at[1], dev(dy=3))
    loop(1, 2, 4)
    to_sibling(1)
    loop(2, 0, 2)
    part = chip_sum(1)
    arrive(r2.at[0], r2_rs.at[0])
    y_src[0, 0:H] = (part[0:H] + r2[0].astype(F32)).astype(BF16)
    y_src[0, H:] = part[H:].astype(BF16)
    send(y_src.at[0], yr.at[0], yr_ss.at[0], yr_rs.at[0], dev(dy=1))
    loop(2, 2, 4)
    to_sibling(2)

    def query_out(xo):
        d = (dqt[:, lanes(xo)] * SCALE).T
        for a in range(2):
            for h in range(4):
                n = a * 4 + h
                dq_src[xo, a, :, h * DIM : (h + 1) * DIM] = d[n * TOK : (n + 1) * TOK].astype(BF16)
        dx = OFF[xo]
        seen = SLOT[(NX - dx) % NX]
        for dc in range(2):
            if (dx, dc) != (0, 0):
                send(dq_src.at[xo, dc], dqr.at[seen, dc], dq_ss.at[xo, dc], dq_rs.at[seen, dc], dev(dx=dx, dc=dc))

    for n, xo in enumerate((3, 1, 2, 0)):
        backward(xo, 0, False)
        query_out(xo)
        if n == 1:
            part = chip_sum(2)
            arrive(r2.at[1], r2_rs.at[1])
            y_src[1, 0:H] = part[0:H].astype(BF16)
            y_src[1, H:] = (part[H:] + r2[1].astype(F32)).astype(BF16)
            send(y_src.at[1], yr.at[1], yr_ss.at[1], yr_rs.at[1], dev(dy=3))
    to_sibling(0)
    part = chip_sum(0)
    for i in range(2):
        arrive(yr.at[i], yr_rs.at[i])
        part += yr[i].astype(F32)
    z_src[...] = part.astype(BF16)
    dkv[0, 0:OWN, :] = part
    for dz in Z_ORDER:
        block = z_src.at[pl.ds(pl.multiple_of(lax.rem(z + dz, NZ) * TOK, TOK), TOK)]
        send(block, zr.at[dz - 1], zr_ss.at[dz], zr_rs.at[dz], dev(dz=dz))

    for dc in range(2):
        total = dq_src[0, 0].astype(F32) if dc == 0 else 0.0
        for slot in range(NX):
            if (slot, dc) != (0, 0):
                arrive(dqr.at[slot, dc], dq_rs.at[slot, dc])
                total += dqr[slot, dc].astype(F32)
        dq_out[:, half(dc)] = total.astype(BF16)
    total = dkv[0, pl.ds(pl.multiple_of(z * TOK, TOK), TOK), :]
    for dz in Z_ORDER:
        arrive(zr.at[dz - 1], zr_rs.at[dz])
        total += zr[dz - 1].astype(F32)
    dk_out[...] = total[:, 0:DIM].astype(BF16)
    dv_out[...] = total[:, DIM:].astype(BF16)
    for copy in pending:
        copy.wait_send()


def body(queries, key_vecs, value_vecs, out_grad):
    vmem, sem = pltpu.VMEM, pltpu.SemaphoreType.DMA
    out = lambda a: jax.ShapeDtypeStruct(a.shape, BF16)
    return pl.pallas_call(
        kernel,
        name="attention_backward",
        out_shape=[out(queries), out(key_vecs), out(value_vecs)],
        in_specs=[pl.BlockSpec(memory_space=vmem)] * 4,
        out_specs=[pl.BlockSpec(memory_space=vmem)] * 3,
        scratch_shapes=[
            vmem((NX, 2, TOK, HALF), BF16),
            vmem((NX, 2, TOK, HALF), BF16),
            vmem((NY, KT, 2 * DIM), BF16),
            vmem((DIM, KEYS), BF16),
            vmem((DIM + 16, KEYS), BF16),
            vmem((KEYS, ROWS), BF16),
            vmem((8, ROWS), F32),
            vmem((DIM + 16, ROWS), F32),
            vmem((NX, 8, RB), F32),
            vmem((NX - 1, NX, 8, RB), F32),
            vmem((8, ROWS), F32),
            vmem((8, ROWS), F32),
            vmem((NX, RB, 128), F32),
            vmem((DIM, ROWS), F32),
            vmem((NY, KT, 2 * DIM), F32),
            vmem((NY, KT // 2, 2 * DIM), BF16),
            vmem((NY, KT // 2, 2 * DIM), BF16),
            vmem((KT // 2, 2 * DIM), BF16),
            vmem((2, KT // 4, 2 * DIM), BF16),
            vmem((2, KT // 2, 2 * DIM), BF16),
            vmem((2, KT // 2, 2 * DIM), BF16),
            vmem((KT // 2, 2 * DIM), BF16),
            vmem((NZ - 1, TOK, 2 * DIM), BF16),
            vmem((NX, 2, TOK, HALF), BF16),
            vmem((NX, 2, TOK, HALF), BF16),
            sem((4,)),
            sem((NX, 2, 2)), sem((NX, 2, 2)),
            sem((NZ,)), sem((NZ,)),
            sem((NY, NZ)), sem((NY, NZ)),
            sem((2, NZ)), sem((2, NZ)),
            sem((NZ,)), sem((NZ,)),
            sem((NX - 1, NX)), sem((NX - 1, NX)),
            sem((NY,)), sem((NY,)),
            sem((2,)), sem((2,)),
            sem((2,)), sem((2,)),
            sem((NZ,)), sem((NZ,)),
            sem((NX, 2)), sem((NX, 2)),
        ],
        compiler_params=pltpu.CompilerParams(
            collective_id=0, has_side_effects=True, vmem_limit_bytes=60 * 2**20
        ),
    )(queries, out_grad, key_vecs, value_vecs)


def solution(mesh):
    spec = P(("ctx", "head"), None)
    return jax.shard_map(
        body, mesh=mesh, in_specs=(spec,) * 4, out_specs=(spec,) * 3, check_vma=False
    )
```

time: 2280 us -> 85.8 us (0.04)
  the two profiles are of different devices: /device:TPU:1 before, /device:TPU:24 now
where the time goes in v1:
time: 85.8 us; the launch traced here: 85.6 us
  Pallas kernels  82 us (96%)
  local copies, waits for them, and re-layouts  2.91 us (3%)
    pallas_call x1, Pallas kernels, body(): pl.pallas_call(kernel, name='attention_backward', out_shape=[out(queries)...  82 us
    unnamed x7, local copies, waits for them, and re-layouts  2.91 us

profile of v1, /device:TPU:24, one launch (start us, length us, event | category | flops | bytes accessed | tf_op | source)
XLA Modules:
  0.0 85.6 jit_solution(14535471507227800191)
XLA Ops:
  0.6 82.0 %attention_backward.1 = (bf16[64,1024]{1,0:T(8,128)(2,1)}, bf16[64,128]{1,0:T(8,128)(2,1)}, bf16[64,128]{1,0:T(8,128)(2,1)}) custom-call(bf16[64,1024]{1,0:T(8,128)(2,1)} %q_in.1, bf16[64,1024]{1,0:T(8,128)(2,1)} %do_in.1, bf16[64,128]{1,0:T(8,128)(2,1)} %k_in.1, bf16[64,128]{1,0:T(8,128)(2,1)} %v_in.1), custom_call_target="tpu_custom_call" | custom-call | tf_op jit(solution)/shard_map/attention_backward/pallas_call | solution.py:334
  82.7 0.0 copy-start.1
  82.7 1.6 %copy.10 = bf16[64,1024]{1,0:T(8,128)(2,1)} copy(bf16[64,1024]{1,0:T(8,128)(2,1)} %get-tuple-element.6) | data formatting | bytes 262144
  84.2 0.0 copy-done.1
  84.2 0.0 copy-start
  84.2 0.6 copy.11
  84.9 0.1 copy-done
  85.0 0.6 copy.12
Async XLA Ops:
  82.7 1.6 %copy-start.1 = (bf16[64,128]{1,0:T(8,128)(2,1)S(1)}, bf16[64,128]{1,0:T(8,128)(2,1)}, u32[]{:S(2)}) copy-start(bf16[64,128]{1,0:T(8,128)(2,1)} %get-tuple-element.7) | copy-start | bytes 49156
  84.2 0.7 copy-start

commit v2 on v1

v2 whole, which is shorter than its diff:
```python
import math

import jax
import jax.numpy as jnp
from jax import lax
from jax.experimental import pallas as pl
from jax.experimental.pallas import tpu as pltpu
from jax.sharding import PartitionSpec as P

F32, BF16 = jnp.float32, jnp.bfloat16
MESH = pl.DeviceIdType.MESH
NX, NY, NZ = 4, 4, 8
TOK = 64
DIM = 128
HALF = 512
RB = 512
KT = 1024
ROWS, KEYS = NX * RB, NY * KT
OFF = (0, 1, 3, 2)
SLOT = (0, 1, 3, 2)
SCALE = DIM**-0.5
LOG2_SCALE = SCALE * math.log2(math.e)
Z_ORDER = (1, 7, 2, 6, 3, 5, 4)
NEAR, FAR = (0, 1, 7, 2), (6, 3, 5, 4)
PLACE = {dz: (h, i) for h, part in enumerate((NEAR, FAR)) for i, dz in enumerate(part)}
SUB = 512


def nt(a, b):
    return lax.dot_general(a, b, (((1,), (1,)), ((), ())), preferred_element_type=F32)


def nn(a, b):
    return jnp.dot(a, b, preferred_element_type=F32)


def kernel(
    q_in, do_in, k_in, v_in, dq_out, dk_out, dv_out,
    qb, dob, kvb, kt, vt, w, sc, mt, acc, st, st_src, sr, lse, rdn, fcol, dqt, dkv,
    sib_src, sib, r2_src, r2, y_src, yr, z_own, z_src, zr, dq_src, dqr,
    loc_sem, q_ss, q_rs, z_ss, z_rs, sb_ss, sb_rs, yk_ss, yk_rs, y2_ss, y2_rs,
    st_ss, st_rs, sib_ss, sib_rs, r2_ss, r2_rs, yr_ss, yr_rs, zr_ss, zr_rs, dq_ss, dq_rs,
):
    ctx, hd = lax.axis_index("ctx"), lax.axis_index("head")
    y, z = ctx // (2 * NZ), lax.rem(ctx // 2, NZ)
    x, c = (hd // 2) * 2 + lax.rem(ctx, 2), lax.rem(hd, 2)

    def dev(dx=0, dy=0, dz=0, dc=0):
        xx, yy = lax.rem(x + dx, NX), lax.rem(y + dy, NY)
        zz, cc = lax.rem(z + dz, NZ), lax.rem(c + dc, 2)
        return ((yy * NZ + zz) * 2 + lax.rem(xx, 2), (xx // 2) * 2 + cc)

    pending = []

    def send(src, dst, ss, rs, to):
        copy = pltpu.make_async_remote_copy(
            src_ref=src, dst_ref=dst, send_sem=ss, recv_sem=rs,
            device_id=to, device_id_type=MESH,
        )
        copy.start()
        pending.append(copy)

    def arrive(ref, rs):
        pltpu.make_async_remote_copy(
            src_ref=ref, dst_ref=ref, send_sem=rs, recv_sem=rs,
            device_id=dev(dc=1), device_id_type=MESH,
        ).wait_recv()

    def half(dc):
        return pl.ds(pl.multiple_of(lax.rem(c + dc, 2) * HALF, HALF), HALF)

    own = [
        pltpu.make_async_copy(k_in, kvb.at[0, 0, 0, 0, :, 0:DIM], loc_sem.at[0]),
        pltpu.make_async_copy(v_in, kvb.at[0, 0, 0, 0, :, DIM : 2 * DIM], loc_sem.at[1]),
        pltpu.make_async_copy(q_in.at[:, half(0)], qb.at[x, 0], loc_sem.at[2]),
        pltpu.make_async_copy(do_in.at[:, half(0)], dob.at[x, 0], loc_sem.at[3]),
    ]
    for copy in own:
        copy.start()
    xc = [(dx, dc) for dx in range(NX) for dc in range(2) if (dx, dc) != (0, 0)]
    partners = [dev(dx=dx, dc=dc) for dx, dc in xc]
    partners += [dev(dz=dz) for dz in range(1, NZ)] + [dev(dy=1), dev(dy=3)]
    barrier = pltpu.get_barrier_semaphore()
    for to in partners:
        pl.semaphore_signal(barrier, inc=1, device_id=to, device_id_type=MESH)
    for copy in own:
        copy.wait()
    pl.semaphore_wait(barrier, len(partners))

    def block(t, dz, core=0):
        h, i = PLACE[dz]
        return kvb.at[t, h, core, i]

    def xat(off):
        return lax.rem(x + off, NX)

    def spread(dz):
        src = block(0, dz)
        send(src, block(2, dz), yk_ss.at[0, dz], yk_rs.at[0, dz], dev(dy=1))
        send(src, block(1, dz), yk_ss.at[1, dz], yk_rs.at[1, dz], dev(dy=3))
        send(src, block(0, dz, 1), sb_ss.at[0, dz], sb_rs.at[0, dz], dev(dc=1))

    for dz in Z_ORDER:
        send(block(0, 0), block(0, dz), z_ss.at[dz], z_rs.at[dz], dev(dz=dz))
    spread(0)
    for dx, dc in ((0, 1), (1, 0), (3, 0), (1, 1), (3, 1), (2, 0), (2, 1)):
        slot = SLOT[(NX - dx) % NX]
        for i, (src, dst) in enumerate(((q_in, qb), (do_in, dob))):
            send(src.at[:, half(dc)], dst.at[x, dc], q_ss.at[dx, dc, i], q_rs.at[slot, dc, i], dev(dx=dx, dc=dc))

    vt[DIM : DIM + 16, :] = jnp.ones((16, KEYS), BF16)
    st[...] = jnp.zeros_like(st)
    for t in range(NY):
        dkv[t] = jnp.zeros((KT, 2 * DIM), F32)
    for dz in Z_ORDER:
        arrive(block(0, dz), z_rs.at[dz])
        spread(dz)

    def keys_of(t, h):
        return kvb[t, h, :, :, :, 0:DIM].reshape(SUB, DIM)

    def values_of(t, h):
        return kvb[t, h, :, :, :, DIM : 2 * DIM].reshape(SUB, DIM)

    def span(t, h):
        return pl.ds(t * KT + h * SUB, SUB)

    def rows_of(ref, xo):
        return jnp.concatenate(
            [ref[xo, a, :, i * DIM : (i + 1) * DIM] for a in range(2) for i in range(4)], axis=0
        )

    def lanes(xo):
        return pl.ds(xo * RB if isinstance(xo, int) else pl.multiple_of(xo * RB, RB), RB)

    def forward(blocks):
        before = None
        for n, now in enumerate(list(blocks) + [None]):
            new_top, total = None, None
            if now is not None:
                qs = rows_of(qb, now[0])
            for i in range(2):
                if now is not None:
                    s = nt(keys_of(*now[1][i]), qs)
                    sc[n % 2, i] = s
                    top = jnp.max(s, axis=0, keepdims=True)
                    new_top = top if new_top is None else jnp.maximum(new_top, top)
                if before is not None:
                    xo, subs, _ = before
                    cols = span(*subs[i])
                    p = jnp.exp2(sc[(n + 1) % 2, i] * LOG2_SCALE - m).astype(BF16)
                    w[cols, lanes(xo)] = p
                    mt[2 * subs[i][0] + subs[i][1], lanes(xo)] = m[0]
                    a = nn(vt[:, cols], p)
                    total = a if total is None else total + a
            if before is not None:
                xo, _, first = before
                if first:
                    st[xo, 0:1, :] = m
                    acc[:, lanes(xo)] = total
                else:
                    old = st[xo, 0:1, :]
                    top = jnp.maximum(old, m)
                    acc[:, lanes(xo)] = acc[:, lanes(xo)] * jnp.exp2(old - top) + total * jnp.exp2(m - top)
                    st[xo, 0:1, :] = top
            if now is not None:
                m = new_top * LOG2_SCALE
            before = now

    def arrive_rows(slot):
        for dc in range(2):
            if (slot, dc) != (0, 0):
                arrive(qb.at[xat(OFF[slot]), dc], q_rs.at[slot, dc, 0])
                arrive(dob.at[xat(OFF[slot]), dc], q_rs.at[slot, dc, 1])

    def arrive_sibling(t, h):
        for dz in (NEAR, FAR)[h]:
            arrive(block(t, dz, 1), sb_rs.at[t, dz])
        kt[:, span(t, h)] = keys_of(t, h).T
        vt[0:DIM, span(t, h)] = values_of(t, h).T

    def from_y(part):
        for n, dz in enumerate(part):
            for i, t in ((0, 2), (1, 1)):
                src = block(t, dz)
                arrive(src, yk_rs.at[i, dz])
                if n % 2 == i:
                    send(src, block(3, dz), y2_ss.at[dz], y2_rs.at[dz], dev(dy=1 if i == 0 else 3))
                send(src, block(t, dz, 1), sb_ss.at[t, dz], sb_rs.at[t, dz], dev(dc=1))

    def from_far_y(part):
        for dz in part:
            src = block(3, dz)
            arrive(src, y2_rs.at[dz])
            send(src, block(3, dz, 1), sb_ss.at[3, dz], sb_rs.at[3, dz], dev(dc=1))

    G0, G1, G2, G3 = ((0, 0), (0, 1)), ((1, 0), (2, 0)), ((1, 1), (2, 1)), ((3, 0), (3, 1))
    from_y(NEAR)
    arrive_rows(0)
    arrive_sibling(0, 0)
    arrive_sibling(0, 1)
    arrive_rows(1)
    arrive_rows(2)
    forward([(xat(off), G0, True) for off in (0, 1, 3)])
    from_y(FAR)
    for t in (1, 2):
        arrive_sibling(t, 0)
    forward([(xat(off), G1, False) for off in (0, 1)])
    from_far_y(NEAR)
    arrive_rows(3)
    forward([(xat(3), G1, False), (xat(2), G0, True), (xat(2), G1, False)])
    from_far_y(FAR)
    for t in (1, 2):
        arrive_sibling(t, 1)
    forward([(xo, G2, False) for xo in range(NX)])
    for h in range(2):
        arrive_sibling(3, h)
    forward([(xo, G3, False) for xo in range(NX)])
    for xo in range(NX):
        rows = lanes(xo)
        grads = rows_of(dob, xo).astype(F32).T
        dot = jnp.sum(grads * acc[0:DIM, rows], axis=0, keepdims=True)
        for i, row in enumerate((st[xo, 0:1, :], acc[DIM : DIM + 1, rows], dot)):
            for j in range(4):
                st_src[xo, 4 * i + j : 4 * i + j + 1, :] = row[:, j * DIM : (j + 1) * DIM]
        for dx in (1, 3, 2):
            seen = SLOT[(NX - dx) % NX] - 1
            send(st_src.at[xo], sr.at[seen, xo], st_ss.at[dx - 1, xo], st_rs.at[seen, xo], dev(dx=dx))

    def totals(xo):
        rows = lanes(xo)
        parts = [st_src[xo]]
        for p in range(3):
            arrive(sr.at[p, xo], st_rs.at[p, xo])
            parts.append(sr[p, xo])
        top = parts[0][0:4]
        for part in parts[1:]:
            top = jnp.maximum(top, part[0:4])
        total, dot = 0.0, 0.0
        for part in parts:
            factor = jnp.exp2(part[0:4] - top)
            total += part[4:8] * factor
            dot += part[8:12] * factor
        wide = lambda a: jnp.concatenate([a[j : j + 1] for j in range(4)], axis=1)
        log_total = wide(top + jnp.log2(total))
        lse[0:1, rows] = log_total
        rdn[0:1, rows] = wide(dot / total)
        f = jnp.exp2(mt[:, rows] - log_total)
        for i in range(RB // 128):
            part = jnp.concatenate([f[:, i * 128 : (i + 1) * 128], jnp.zeros((120, 128), F32)], axis=0)
            fcol[xo, i * 128 : (i + 1) * 128, :] = part.T

    def backward(xo, t, h, start=False):
        rows = lanes(xo)
        sub = 2 * t + h
        f = jnp.exp2(mt[sub : sub + 1, rows] - lse[0:1, rows])
        grads = (rows_of(dob, xo).astype(F32) * fcol[xo, :, sub : sub + 1]).astype(BF16)
        p = w[span(t, h), rows]
        pg = nt(values_of(t, h), grads) - f * rdn[0:1, rows]
        ds = p * pg.astype(BF16)
        part = pl.ds(h * SUB, SUB)
        dkv[t, part, DIM : 2 * DIM] += nn(p, grads)
        dkv[t, part, 0:DIM] += nn(ds, rows_of(qb, xo))
        d = nn(kt[:, span(t, h)], ds)
        if start:
            dqt[:, rows] = d
        else:
            dqt[:, rows] += d

    OWN = SUB // 2
    factor = jnp.where(lax.broadcasted_iota(jnp.int32, (1, 2 * DIM), 1) < DIM, SCALE, 1.0)

    def to_sibling(t, h):
        sib_src[t, h] = (dkv[t, h * SUB + OWN : (h + 1) * SUB, :] * factor).astype(BF16)
        send(sib_src.at[t, h], sib.at[t, h], sib_ss.at[t, h], sib_rs.at[t, h], dev(dc=1))

    def chip_sum(t, h):
        arrive(sib.at[t, h], sib_rs.at[t, h])
        return dkv[t, h * SUB : h * SUB + OWN, :] * factor + sib[t, h].astype(F32)

    def to_far_y(h):
        r2_src[h] = chip_sum(3, h).reshape(2, OWN // 2, 2 * DIM).astype(BF16)
        for i in range(2):
            send(r2_src.at[h, i], r2.at[h, i], r2_ss.at[h, i], r2_rs.at[h, i], dev(dy=1 if i == 0 else 3))

    def to_y(t, h):
        i = t - 1
        part = chip_sum(t, h)
        arrive(r2.at[h, i], r2_rs.at[h, i])
        more = r2[h, i].astype(F32)
        lo, hi = part[0 : OWN // 2], part[OWN // 2 :]
        lo, hi = (lo + more, hi) if i == 0 else (lo, hi + more)
        y_src[i, h, 0 : OWN // 2] = lo.astype(BF16)
        y_src[i, h, OWN // 2 :] = hi.astype(BF16)
        send(y_src.at[i, h], yr.at[i, h], yr_ss.at[i, h], yr_rs.at[i, h], dev(dy=1 if t == 1 else 3))

    def half_tile(t, h):
        for xo in range(NX):
            backward(xo, t, h)
        to_sibling(t, h)

    for xo in range(NX):
        totals(xo)
        backward(xo, 3, 1, True)
    to_sibling(3, 1)
    half_tile(3, 0)
    to_far_y(1)
    half_tile(1, 1)
    to_far_y(0)
    half_tile(2, 1)
    to_y(1, 1)
    half_tile(1, 0)
    to_y(2, 1)
    half_tile(2, 0)
    to_y(1, 0)
    half_tile(0, 1)
    to_y(2, 0)

    def query_out(slot):
        dx = OFF[slot]
        d = (dqt[:, lanes(xat(dx))] * SCALE).T
        for a in range(2):
            for i in range(4):
                n = a * 4 + i
                dq_src[slot, a, :, i * DIM : (i + 1) * DIM] = d[n * TOK : (n + 1) * TOK].astype(BF16)
        seen = SLOT[(NX - dx) % NX]
        for dc in range(2):
            if (dx, dc) != (0, 0):
                send(dq_src.at[slot, dc], dqr.at[seen, dc], dq_ss.at[slot, dc], dq_rs.at[seen, dc], dev(dx=dx, dc=dc))

    def to_z(h):
        part = chip_sum(0, h)
        for i in range(2):
            arrive(yr.at[i, h], yr_rs.at[i, h])
            part += yr[i, h].astype(F32)
        if h == 0:
            z_own[...] = part[0:TOK]
        z_src[h] = part.astype(BF16).reshape(4, TOK, 2 * DIM)
        for dz in reversed((NEAR[1:], FAR)[h]):
            send(z_src.at[h, PLACE[dz][1]], zr.at[dz - 1], zr_ss.at[dz], zr_rs.at[dz], dev(dz=NZ - dz))

    for n, slot in enumerate((3, 1, 2, 0)):
        backward(xat(OFF[slot]), 0, 0)
        query_out(slot)
        if n == 2:
            to_z(1)
    to_sibling(0, 0)
    to_z(0)

    for dc in range(2):
        total = dq_src[0, 0].astype(F32) if dc == 0 else 0.0
        for slot in range(NX):
            if (slot, dc) != (0, 0):
                arrive(dqr.at[slot, dc], dq_rs.at[slot, dc])
                total += dqr[slot, dc].astype(F32)
        dq_out[:, half(dc)] = total.astype(BF16)
    total = z_own[...]
    for dz in reversed(Z_ORDER):
        arrive(zr.at[dz - 1], zr_rs.at[dz])
        total += zr[dz - 1].astype(F32)
    dk_out[...] = total[:, 0:DIM].astype(BF16)
    dv_out[...] = total[:, DIM:].astype(BF16)
    for copy in pending:
        copy.wait_send()


def body(queries, key_vecs, value_vecs, out_grad):
    vmem, sem = pltpu.VMEM, pltpu.SemaphoreType.DMA
    out = lambda a: jax.ShapeDtypeStruct(a.shape, BF16)
    return pl.pallas_call(
        kernel,
        name="attention_backward",
        out_shape=[out(queries), out(key_vecs), out(value_vecs)],
        in_specs=[pl.BlockSpec(memory_space=pl.ANY)] * 4,
        out_specs=[pl.BlockSpec(memory_space=vmem)] * 3,
        scratch_shapes=[
            vmem((NX, 2, TOK, HALF), BF16),
            vmem((NX, 2, TOK, HALF), BF16),
            vmem((NY, 2, 2, NZ // 2, TOK, 2 * DIM), BF16),
            vmem((DIM, KEYS), BF16),
            vmem((DIM + 16, KEYS), BF16),
            vmem((KEYS, ROWS), BF16),
            vmem((2, 2, SUB, RB), F32),
            vmem((8, ROWS), F32),
            vmem((DIM + 16, ROWS), F32),
            vmem((NX, 8, RB), F32),
            vmem((NX, 16, 128), F32),
            vmem((NX - 1, NX, 16, 128), F32),
            vmem((8, ROWS), F32),
            vmem((8, ROWS), F32),
            vmem((NX, RB, 128), F32),
            vmem((DIM, ROWS), F32),
            vmem((NY, KT, 2 * DIM), F32),
            vmem((NY, 2, KT // 4, 2 * DIM), BF16),
            vmem((NY, 2, KT // 4, 2 * DIM), BF16),
            vmem((2, 2, KT // 8, 2 * DIM), BF16),
            vmem((2, 2, KT // 8, 2 * DIM), BF16),
            vmem((2, 2, KT // 4, 2 * DIM), BF16),
            vmem((2, 2, KT // 4, 2 * DIM), BF16),
            vmem((TOK, 2 * DIM), F32),
            vmem((2, NZ // 2, TOK, 2 * DIM), BF16),
            vmem((NZ - 1, TOK, 2 * DIM), BF16),
            vmem((NX, 2, TOK, HALF), BF16),
            vmem((NX, 2, TOK, HALF), BF16),
            sem((4,)),
            sem((NX, 2, 2)), sem((NX, 2, 2)),
            sem((NZ,)), sem((NZ,)),
            sem((NY, NZ)), sem((NY, NZ)),
            sem((2, NZ)), sem((2, NZ)),
            sem((NZ,)), sem((NZ,)),
            sem((NX - 1, NX)), sem((NX - 1, NX)),
            sem((NY, 2)), sem((NY, 2)),
            sem((2, 2)), sem((2, 2)),
            sem((2, 2)), sem((2, 2)),
            sem((NZ,)), sem((NZ,)),
            sem((NX, 2)), sem((NX, 2)),
        ],
        compiler_params=pltpu.CompilerParams(
            collective_id=0, has_side_effects=True, vmem_limit_bytes=60 * 2**20
        ),
    )(queries, out_grad, key_vecs, value_vecs)


def solution(mesh):
    spec = P(("ctx", "head"), None)
    return jax.shard_map(
        body, mesh=mesh, in_specs=(spec,) * 4, out_specs=(spec,) * 3, check_vma=False
    )
```

time: 85.8 us -> 71.9 us (0.84)
  the two profiles are of different devices: /device:TPU:24 before, /device:TPU:1 now
where the time goes in v2:
time: 71.9 us; the launch traced here: 71.7 us
  Pallas kernels  68.1 us (95%)
  local copies, waits for them, and re-layouts  2.91 us (4%)
    pallas_call x1, Pallas kernels, body(): pl.pallas_call(kernel, name='attention_backward', out_shape=[out(queries)...  68.1 us
    unnamed x7, local copies, waits for them, and re-layouts  2.91 us

profile of v2, /device:TPU:1, one launch (start us, length us, event | category | flops | bytes accessed | tf_op | source)
XLA Modules:
  0.0 71.7 jit_solution(12416069574285396203)
XLA Ops:
  0.6 68.1 %attention_backward.1 = (bf16[64,1024]{1,0:T(8,128)(2,1)}, bf16[64,128]{1,0:T(8,128)(2,1)}, bf16[64,128]{1,0:T(8,128)(2,1)}) custom-call(bf16[64,1024]{1,0:T(8,128)(2,1)} %q_in.1, bf16[64,1024]{1,0:T(8,128)(2,1)} %do_in.1, bf16[64,128]{1,0:T(8,128)(2,1)} %k_in.1, bf16[64,128]{1,0:T(8,128)(2,1)} %v_in.1), custom_call_target="tpu_custom_call" | custom-call | tf_op jit(solution)/shard_map/attention_backward/pallas_call | solution.py:370
  68.8 0.0 copy-start.1
  68.8 1.6 %copy.10 = bf16[64,1024]{1,0:T(8,128)(2,1)} copy(bf16[64,1024]{1,0:T(8,128)(2,1)} %get-tuple-element.6) | data formatting | bytes 262144
  70.3 0.0 copy-done.1
  70.3 0.0 copy-start
  70.3 0.6 copy.11
  70.9 0.1 copy-done
  71.1 0.6 copy.12
Async XLA Ops:
  68.8 1.6 %copy-start.1 = (bf16[64,128]{1,0:T(8,128)(2,1)S(1)}, bf16[64,128]{1,0:T(8,128)(2,1)}, u32[]{:S(2)}) copy-start(bf16[64,128]{1,0:T(8,128)(2,1)} %get-tuple-element.7) | copy-start | bytes 49156
  70.3 0.7 %copy-start = (bf16[64,128]{1,0:T(8,128)(2,1)S(1)}, bf16[64,128]{1,0:T(8,128)(2,1)}, u32[]{:S(2)}) copy-start(bf16[64,128]{1,0:T(8,128)(2,1)} %get-tuple-element.8) | copy-start | bytes 49156

commit v3 on v2

--- a/solution.py
+++ b/solution.py
@@ -133,7 +133,7 @@
     def lanes(xo):
         return pl.ds(xo * RB if isinstance(xo, int) else pl.multiple_of(xo * RB, RB), RB)
 
-    def forward(blocks):
+    def forward(blocks, finished=None):
         before = None
         for n, now in enumerate(list(blocks) + [None]):
             new_top, total = None, None
@@ -163,6 +163,8 @@
                     top = jnp.maximum(old, m)
                     acc[:, lanes(xo)] = acc[:, lanes(xo)] * jnp.exp2(old - top) + total * jnp.exp2(m - top)
                     st[xo, 0:1, :] = top
+                if finished is not None:
+                    finished(xo)
             if now is not None:
                 m = new_top * LOG2_SCALE
             before = now
@@ -215,8 +217,8 @@
     forward([(xo, G2, False) for xo in range(NX)])
     for h in range(2):
         arrive_sibling(3, h)
-    forward([(xo, G3, False) for xo in range(NX)])
-    for xo in range(NX):
+
+    def exchange(xo):
         rows = lanes(xo)
         grads = rows_of(dob, xo).astype(F32).T
         dot = jnp.sum(grads * acc[0:DIM, rows], axis=0, keepdims=True)
@@ -226,6 +228,8 @@
         for dx in (1, 3, 2):
             seen = SLOT[(NX - dx) % NX] - 1
             send(st_src.at[xo], sr.at[seen, xo], st_ss.at[dx - 1, xo], st_rs.at[seen, xo], dev(dx=dx))
+
+    forward([(xo, G3, False) for xo in range(NX)], exchange)
 
     def totals(xo):
         rows = lanes(xo)
@@ -318,11 +322,11 @@
 
     def query_out(slot):
         dx = OFF[slot]
-        d = (dqt[:, lanes(xat(dx))] * SCALE).T
+        d = (dqt[:, lanes(xat(dx))] * SCALE).astype(BF16).T
         for a in range(2):
             for i in range(4):
                 n = a * 4 + i
-                dq_src[slot, a, :, i * DIM : (i + 1) * DIM] = d[n * TOK : (n + 1) * TOK].astype(BF16)
+                dq_src[slot, a, :, i * DIM : (i + 1) * DIM] = d[n * TOK : (n + 1) * TOK]
         seen = SLOT[(NX - dx) % NX]
         for dc in range(2):
             if (dx, dc) != (0, 0):
@@ -339,12 +343,13 @@
         for dz in reversed((NEAR[1:], FAR)[h]):
             send(z_src.at[h, PLACE[dz][1]], zr.at[dz - 1], zr_ss.at[dz], zr_rs.at[dz], dev(dz=NZ - dz))
 
-    for n, slot in enumerate((3, 1, 2, 0)):
+    for slot in (3, 1, 2):
         backward(xat(OFF[slot]), 0, 0)
         query_out(slot)
-        if n == 2:
-            to_z(1)
+    backward(xat(0), 0, 0)
     to_sibling(0, 0)
+    to_z(1)
+    query_out(0)
     to_z(0)
 
     for dc in range(2):
@@ -366,7 +371,7 @@
 
 def body(queries, key_vecs, value_vecs, out_grad):
     vmem, sem = pltpu.VMEM, pltpu.SemaphoreType.DMA
-    out = lambda a: jax.ShapeDtypeStruct(a.shape, BF16)
+    out = lambda a: vmem(a.shape, BF16)
     return pl.pallas_call(
         kernel,
         name="attention_backward",

time: 71.9 us -> 69 us (0.960)
  Pallas kernels: 68.1 us -> 66.4 us
  local copies, waits for them, and re-layouts: 2.91 us -> 1.87 us
    pallas_call x1, Pallas kernels: 68.1 us -> 66.4 us  [body(): pl.pallas_call(kernel, name='attention_backward', out_shape=[out(queries)...]
    unnamed x7 -> x3, local copies, waits for them, and re-layouts: 2.91 us -> 1.87 us
where the time goes in v3:
time: 69 us; the launch traced here: 68.9 us
  Pallas kernels  66.4 us (96%)
  local copies, waits for them, and re-layouts  1.87 us (3%)
    pallas_call x1, Pallas kernels, body(): pl.pallas_call(kernel, name='attention_backward', out_shape=[out(queries)...  66.4 us
    unnamed x3, local copies, waits for them, and re-layouts  1.87 us

profile of v3, /device:TPU:1, one launch (start us, length us, event | category | flops | bytes accessed | tf_op | source)
XLA Modules:
  0.0 68.9 jit_solution(2047883239735476616)
XLA Ops:
  0.6 66.4 %attention_backward.1 = (bf16[64,1024]{1,0:T(8,128)(2,1)S(1)}, bf16[64,128]{1,0:T(8,128)(2,1)S(1)}, bf16[64,128]{1,0:T(8,128)(2,1)S(1)}) custom-call(bf16[64,1024]{1,0:T(8,128)(2,1)} %q_in.1, bf16[64,1024]{1,0:T(8,128)(2,1)} %do_in.1, bf16[64,128]{1,0:T(8,128)(2,1)} %k_in.1, bf16[64,128]{1,0:T(8,128)(2,1)} %v_in.1), custom_call_target="tpu_custom_call" | custom-call | tf_op jit(solution)/shard_map/attention_backward/pallas_call | solution.py:375
  67.0 0.7 copy.10
  67.7 0.6 copy.11
  68.3 0.6 copy.12

commit v4 on v3

--- a/solution.py
+++ b/solution.py
@@ -35,8 +35,8 @@
 
 
 def kernel(
-    q_in, do_in, k_in, v_in, dq_out, dk_out, dv_out,
-    qb, dob, kvb, kt, vt, w, sc, mt, acc, st, st_src, sr, lse, rdn, fcol, dqt, dkv,
+    q_in, do_in, k_in, v_in, dq_out, dkv_out,
+    qb, dob, kvb, kt, vt, w, sc, dot_t, scaled, mt, acc, st, st_src, sr, lse, rdn, fcol, dqt, dkv,
     sib_src, sib, r2_src, r2, y_src, yr, z_own, z_src, zr, dq_src, dqr,
     loc_sem, q_ss, q_rs, z_ss, z_rs, sb_ss, sb_rs, yk_ss, yk_rs, y2_ss, y2_rs,
     st_ss, st_rs, sib_ss, sib_rs, r2_ss, r2_rs, yr_ss, yr_rs, zr_ss, zr_rs, dq_ss, dq_rs,
@@ -108,10 +108,27 @@
         for i, (src, dst) in enumerate(((q_in, qb), (do_in, dob))):
             send(src.at[:, half(dc)], dst.at[x, dc], q_ss.at[dx, dc, i], q_rs.at[slot, dc, i], dev(dx=dx, dc=dc))
 
+    def rows_of(ref, xo):
+        return jnp.concatenate(
+            [ref[xo, a, :, i * DIM : (i + 1) * DIM] for a in range(2) for i in range(4)], axis=0
+        )
+
+    def lanes(xo):
+        return pl.ds(xo * RB if isinstance(xo, int) else pl.multiple_of(xo * RB, RB), RB)
+
+    def arrive_rows(slot):
+        xo = xat(OFF[slot])
+        for dc in range(2):
+            if (slot, dc) != (0, 0):
+                arrive(qb.at[xo, dc], q_rs.at[slot, dc, 0])
+                arrive(dob.at[xo, dc], q_rs.at[slot, dc, 1])
+        dot_t[:, lanes(xo)] = rows_of(dob, xo).T
+
     vt[DIM : DIM + 16, :] = jnp.ones((16, KEYS), BF16)
     st[...] = jnp.zeros_like(st)
     for t in range(NY):
         dkv[t] = jnp.zeros((KT, 2 * DIM), F32)
+    arrive_rows(0)
     for dz in Z_ORDER:
         arrive(block(0, dz), z_rs.at[dz])
         spread(dz)
@@ -124,14 +141,6 @@
 
     def span(t, h):
         return pl.ds(t * KT + h * SUB, SUB)
-
-    def rows_of(ref, xo):
-        return jnp.concatenate(
-            [ref[xo, a, :, i * DIM : (i + 1) * DIM] for a in range(2) for i in range(4)], axis=0
-        )
-
-    def lanes(xo):
-        return pl.ds(xo * RB if isinstance(xo, int) else pl.multiple_of(xo * RB, RB), RB)
 
     def forward(blocks, finished=None):
         before = None
@@ -169,12 +178,6 @@
                 m = new_top * LOG2_SCALE
             before = now
 
-    def arrive_rows(slot):
-        for dc in range(2):
-            if (slot, dc) != (0, 0):
-                arrive(qb.at[xat(OFF[slot]), dc], q_rs.at[slot, dc, 0])
-                arrive(dob.at[xat(OFF[slot]), dc], q_rs.at[slot, dc, 1])
-
     def arrive_sibling(t, h):
         for dz in (NEAR, FAR)[h]:
             arrive(block(t, dz, 1), sb_rs.at[t, dz])
@@ -198,11 +201,10 @@
 
     G0, G1, G2, G3 = ((0, 0), (0, 1)), ((1, 0), (2, 0)), ((1, 1), (2, 1)), ((3, 0), (3, 1))
     from_y(NEAR)
-    arrive_rows(0)
     arrive_sibling(0, 0)
-    arrive_sibling(0, 1)
     arrive_rows(1)
     arrive_rows(2)
+    arrive_sibling(0, 1)
     forward([(xat(off), G0, True) for off in (0, 1, 3)])
     from_y(FAR)
     for t in (1, 2):
@@ -220,8 +222,7 @@
 
     def exchange(xo):
         rows = lanes(xo)
-        grads = rows_of(dob, xo).astype(F32).T
-        dot = jnp.sum(grads * acc[0:DIM, rows], axis=0, keepdims=True)
+        dot = jnp.sum(dot_t[:, rows].astype(F32) * acc[0:DIM, rows], axis=0, keepdims=True)
         for i, row in enumerate((st[xo, 0:1, :], acc[DIM : DIM + 1, rows], dot)):
             for j in range(4):
                 st_src[xo, 4 * i + j : 4 * i + j + 1, :] = row[:, j * DIM : (j + 1) * DIM]
@@ -258,7 +259,11 @@
         rows = lanes(xo)
         sub = 2 * t + h
         f = jnp.exp2(mt[sub : sub + 1, rows] - lse[0:1, rows])
-        grads = (rows_of(dob, xo).astype(F32) * fcol[xo, :, sub : sub + 1]).astype(BF16)
+        if (t, h) in ((3, 1), (1, 1), (1, 0), (0, 1)):
+            grads = (rows_of(dob, xo).astype(F32) * fcol[xo, :, sub : sub + 1]).astype(BF16)
+            scaled[rows, :] = grads
+        else:
+            grads = scaled[rows, :]
         p = w[span(t, h), rows]
         pg = nt(values_of(t, h), grads) - f * rdn[0:1, rows]
         ds = p * pg.astype(BF16)
@@ -363,21 +368,19 @@
     for dz in reversed(Z_ORDER):
         arrive(zr.at[dz - 1], zr_rs.at[dz])
         total += zr[dz - 1].astype(F32)
-    dk_out[...] = total[:, 0:DIM].astype(BF16)
-    dv_out[...] = total[:, DIM:].astype(BF16)
+    dkv_out[...] = total
     for copy in pending:
         copy.wait_send()
 
 
 def body(queries, key_vecs, value_vecs, out_grad):
     vmem, sem = pltpu.VMEM, pltpu.SemaphoreType.DMA
-    out = lambda a: vmem(a.shape, BF16)
-    return pl.pallas_call(
+    query_grad, both = pl.pallas_call(
         kernel,
         name="attention_backward",
-        out_shape=[out(queries), out(key_vecs), out(value_vecs)],
+        out_shape=[vmem(queries.shape, BF16), vmem((TOK, 2 * DIM), F32)],
         in_specs=[pl.BlockSpec(memory_space=pl.ANY)] * 4,
-        out_specs=[pl.BlockSpec(memory_space=vmem)] * 3,
+        out_specs=[pl.BlockSpec(memory_space=vmem)] * 2,
         scratch_shapes=[
             vmem((NX, 2, TOK, HALF), BF16),
             vmem((NX, 2, TOK, HALF), BF16),
@@ -386,6 +389,8 @@
             vmem((DIM + 16, KEYS), BF16),
             vmem((KEYS, ROWS), BF16),
             vmem((2, 2, SUB, RB), F32),
+            vmem((DIM, ROWS), BF16),
+            vmem((ROWS, DIM), BF16),
             vmem((8, ROWS), F32),
             vmem((DIM + 16, ROWS), F32),
             vmem((NX, 8, RB), F32),
@@ -424,6 +429,7 @@
             collective_id=0, has_side_effects=True, vmem_limit_bytes=60 * 2**20
         ),
     )(queries, out_grad, key_vecs, value_vecs)
+    return query_grad, both[:, :DIM].astype(BF16), both[:, DIM:].astype(BF16)
 
 
 def solution(mesh):

time: 69 us -> 67.9 us (0.984)
    unnamed x3 -> x1, local copies, waits for them, and re-layouts: 1.87 us -> 0.65 us
where the time goes in v4:
time: 67.9 us; the launch traced here: 67.8 us
  Pallas kernels  65.8 us (97%)
  local copies, waits for them, and re-layouts  1.27 us (2%)
    pallas_call x1, Pallas kernels, body(): pl.pallas_call(kernel, name='attention_backward', out_shape=[vmem(queries...  65.8 us

profile of v4, /device:TPU:1, one launch (start us, length us, event | category | flops | bytes accessed | tf_op | source)
XLA Modules:
  0.0 67.8 jit_solution(12313451582896975288)
XLA Ops:
  0.6 65.8 %attention_backward.1 = (bf16[64,1024]{1,0:T(8,128)(2,1)S(1)}, f32[64,256]{1,0:T(8,128)S(1)}) custom-call(bf16[64,1024]{1,0:T(8,128)(2,1)} %q_in.1, bf16[64,1024]{1,0:T(8,128)(2,1)} %do_in.1, bf16[64,128]{1,0:T(8,128)(2,1)} %k_in.1, bf16[64,128]{1,0:T(8,128)(2,1)} %v_in.1), custom_call_target="tpu_custom_call" | custom-call | tf_op jit(solution)/shard_map/attention_backward/pallas_call | solution.py:378
  66.5 0.6 fusion
  67.1 0.7 copy.8
  (1 shorter events, 0.0 us)

commit v5 on v4

--- a/solution.py
+++ b/solution.py
@@ -75,14 +75,14 @@
         pltpu.make_async_copy(q_in.at[:, half(0)], qb.at[x, 0], loc_sem.at[2]),
         pltpu.make_async_copy(do_in.at[:, half(0)], dob.at[x, 0], loc_sem.at[3]),
     ]
-    for copy in own:
-        copy.start()
     xc = [(dx, dc) for dx in range(NX) for dc in range(2) if (dx, dc) != (0, 0)]
     partners = [dev(dx=dx, dc=dc) for dx, dc in xc]
-    partners += [dev(dz=dz) for dz in range(1, NZ)] + [dev(dy=1), dev(dy=3)]
+    partners = [dev(dz=dz) for dz in (4, 3, 5, 2, 6, 1, 7)] + partners[::-1] + [dev(dy=1), dev(dy=3)]
     barrier = pltpu.get_barrier_semaphore()
     for to in partners:
         pl.semaphore_signal(barrier, inc=1, device_id=to, device_id_type=MESH)
+    for copy in own:
+        copy.start()
     for copy in own:
         copy.wait()
     pl.semaphore_wait(barrier, len(partners))
@@ -348,6 +348,7 @@
         for dz in reversed((NEAR[1:], FAR)[h]):
             send(z_src.at[h, PLACE[dz][1]], zr.at[dz - 1], zr_ss.at[dz], zr_rs.at[dz], dev(dz=NZ - dz))
 
+    gone = len(pending)
     for slot in (3, 1, 2):
         backward(xat(OFF[slot]), 0, 0)
         query_out(slot)
@@ -356,6 +357,8 @@
     to_z(1)
     query_out(0)
     to_z(0)
+    for copy in pending[:gone]:
+        copy.wait_send()
 
     for dc in range(2):
         total = dq_src[0, 0].astype(F32) if dc == 0 else 0.0
@@ -369,7 +372,7 @@
         arrive(zr.at[dz - 1], zr_rs.at[dz])
         total += zr[dz - 1].astype(F32)
     dkv_out[...] = total
-    for copy in pending:
+    for copy in pending[gone:]:
         copy.wait_send()
 
 

time: 67.9 us -> 67.4 us (level)
  no operation moved by 1% of the time
where the time goes in v5:
time: 67.4 us; the launch traced here: 67.3 us
  Pallas kernels  65.3 us (97%)
  local copies, waits for them, and re-layouts  1.27 us (2%)
    pallas_call x1, Pallas kernels, body(): pl.pallas_call(kernel, name='attention_backward', out_shape=[vmem(queries...  65.3 us

profile of v5, /device:TPU:1, one launch (start us, length us, event | category | flops | bytes accessed | tf_op | source)
XLA Modules:
  0.0 67.3 jit_solution(9751677551122369418)
XLA Ops:
  0.6 65.3 %attention_backward.1 = (bf16[64,1024]{1,0:T(8,128)(2,1)S(1)}, f32[64,256]{1,0:T(8,128)S(1)}) custom-call(bf16[64,1024]{1,0:T(8,128)(2,1)} %q_in.1, bf16[64,1024]{1,0:T(8,128)(2,1)} %do_in.1, bf16[64,128]{1,0:T(8,128)(2,1)} %k_in.1, bf16[64,128]{1,0:T(8,128)(2,1)} %v_in.1), custom_call_target="tpu_custom_call" | custom-call | tf_op jit(solution)/shard_map/attention_backward/pallas_call | solution.py:381
  66.0 0.6 fusion
  66.6 0.7 copy.8
  (1 shorter events, 0.0 us)
